TPU v7x, 256 devices: a whole 4x4x8 slice. The times are simulated.
256 devices in a mesh: shard: 64 (over x, z, core), dp: 4 (over y).
Axes of the slice: x: 4, y: 4, z: 8, core: 2. Of those that a mesh axis runs over, the one named last changes fastest.
Arguments:
- grads: bfloat16 [4, 2, 7936, 3968], P('dp', None, 'shard'), may hold values from -100 to 100
- errors: bfloat16 [4, 2, 7936, 3968], P('dp', None, 'shard'), may hold values from -4 to 4
- q_init: float32 [2, 32, 3968], replicated, may hold values from -6 to 6
Outputs:
- update: float32 [2, 7936, 3968], P(None, 'shard')
- new_errors: bfloat16 [4, 2, 7936, 3968], P('dp', None, 'shard')
- q_next: float32 [2, 32, 3968], replicated
All inputs are finite; a program needn't handle non-finite values.
Results may differ from a plain program's by a relative error of at most 0.001.
Values sent between devices are 32-bit elements; how exact they have to be, the bound alone decides.
A program may use at most 64 MiB of HBM per device.

v0:
```python
import functools

import jax
import jax.numpy as jnp
from jax import lax
from jax.experimental import pallas as pl
from jax.experimental.pallas import tpu as pltpu
from jax.sharding import PartitionSpec as P

MESH = pl.DeviceIdType.MESH
BF = jnp.bfloat16
F32 = jnp.float32
HIGH = lax.Precision.HIGHEST

ROWS, D, RANK = 124, 3968, 32
BOTH = 2 * ROWS
PAD = 4096
HALF, CHUNK = PAD // 2, 128
GROUPS = ((0, 1024), (1024, 1024), (2048, 1024), (3072, 896))
EPS = 1e-06


def nt(a, b, precision=None):
    return lax.dot_general(
        a, b, (((1,), (1,)), ((), ())), precision=precision, preferred_element_type=F32
    )


def nn(a, b, precision=None):
    return lax.dot_general(
        a, b, (((1,), (0,)), ((), ())), precision=precision, preferred_element_type=F32
    )


def two_terms(v):
    hi = v.astype(BF)
    return hi, (v - hi.astype(F32)).astype(BF)


def by_layer(even, odd):
    col = lax.broadcasted_iota(jnp.int32, even.shape, 1)
    return jnp.where(col % 2 == 0, even, odd)


def masked_pair(even, odd):
    zero = jnp.zeros_like(even)
    return jnp.concatenate([by_layer(even, zero), by_layer(zero, odd)], axis=0)


def gram_schmidt(gram):
    n = gram.shape[0]
    row = lax.broadcasted_iota(jnp.int32, (n, n), 0)
    col = lax.broadcasted_iota(jnp.int32, (n, n), 1)
    w, z = gram, gram
    t = jnp.where(row == col, 1.0, 0.0).astype(F32)
    scale = jnp.zeros((n, n), F32)
    for j in range(n):
        zcol = jnp.broadcast_to(z[:, j : j + 1], (n, n))
        wcol = jnp.broadcast_to(w[:, j : j + 1], (n, n))
        norm = jnp.maximum(zcol[j : j + 1, :], 0.0)
        s = lax.rsqrt(norm + EPS)
        scale = jnp.where(row == j, s, scale)
        if j + 1 < n:
            u = s * s
            wrow, zrow, trow = w[j : j + 1, :] * u, z[j : j + 1, :] * u, t[j : j + 1, :] * u
            z = z - wcol * (zrow - wrow * (norm * u)) - zcol * wrow
            w = w - wcol * wrow
            t = t - jnp.where(row > j, wcol, 0.0) * trow
    return t * scale


def reduce_kernel(
    g_ref, e_ref, q_ref,
    gs, es, bc, qn,
    qs, pslots, gl, gcore, gx, gz, tt, rloc, rcore, rs, slots, zslots,
    in_sem, psem_s, psem_r, gsem_s, gsem_r, csem_s, csem_r, rsem_s, rsem_r, zsem_s, zsem_r, asem_s, asem_r, qsem_s, qsem_r,
):
    shard, y = lax.axis_index("shard"), lax.axis_index("dp")
    core = lax.rem(shard, 2)
    z = lax.rem(lax.div(shard, 2), 8)
    x = lax.div(shard, 16)

    def dev(x_, y_, z_, c_):
        return ((x_ * 8 + z_) * 2 + c_, y_)

    sibling = dev(x, y, z, 1 - core)
    xs = [lax.rem(x + d, 4) for d in range(4)]
    ys = [lax.rem(y + d, 4) for d in range(4)]
    zs = [lax.rem(z + d, 8) for d in range(8)]
    plane = [(i, j) for i in (2, 3, 1, 0) for j in (2, 3, 1, 0) if i or j]
    me = x * 4 + y

    barrier = pltpu.get_barrier_semaphore()
    partners = [sibling]
    partners += [dev(xs[i], ys[j], z, core) for i, j in plane]
    partners += [dev(x, y, zs[d], core) for d in range(1, 8)]

    gs[BOTH - 8 : 256, :] = jnp.zeros((16, PAD), BF)
    es[BOTH - 8 : 256, :] = jnp.zeros((16, PAD), BF)
    g_rows, e_rows = g_ref.reshape(BOTH, D), e_ref.reshape(BOTH, D)
    load_q = pltpu.make_async_copy(q_ref, qs, in_sem.at[8])
    load_q.start()
    loads = []
    for b, (c0, w) in enumerate(GROUPS):
        cols, rows = pl.ds(c0, w), pl.ds(0, BOTH)
        pair = [
            pltpu.make_async_copy(g_rows.at[:, cols], gs.at[rows, cols], in_sem.at[b]),
            pltpu.make_async_copy(e_rows.at[:, cols], es.at[rows, cols], in_sem.at[4 + b]),
        ]
        for cp in pair:
            cp.start()
        loads.append(pair)
    for p in partners:
        pl.semaphore_signal(barrier, inc=1, device_id=p, device_id_type=MESH)
    gs[:, D:PAD] = jnp.zeros((256, PAD - D), BF)
    es[:, D:PAD] = jnp.zeros((256, PAD - D), BF)

    both = None
    load_q.wait()
    for b, (c0, w) in enumerate(GROUPS):
        for cp in loads[b]:
            cp.wait()

        terms = jnp.concatenate(two_terms(qs[:, :, c0 : c0 + w].reshape(2 * RANK, w)), axis=0)
        part = nt(terms, gs[:, c0 : c0 + w]) + nt(terms, es[:, c0 : c0 + w])
        both = part if both is None else both + part
    both = both[:64] + both[64:]
    pslots[y] = by_layer(both[:RANK], both[RANK:])

    pl.semaphore_wait(barrier, len(partners))

    def remote(src, dst, send, recv, device):
        return pltpu.make_async_remote_copy(
            src_ref=src, dst_ref=dst, send_sem=send, recv_sem=recv, device_id=device, device_id_type=MESH
        )

    def arrived(dst, sem):
        remote(dst, dst, sem, sem, sibling).wait_recv()

    def left(src, sem):
        remote(src, src, sem, sem, sibling).wait_send()

    def send(src, dst, s, r, device):
        remote(src, dst, s, r, device).start()

    for d in (2, 1, 3):
        send(pslots.at[y], pslots.at[y], psem_s.at[0], psem_r.at[0], dev(x, ys[d], z, core))
    arrived(pslots.at[pl.ds(0, 3)], psem_r.at[0])
    pt = (pslots[0] + pslots[1]) + (pslots[2] + pslots[3])
    pm = masked_pair(pt, pt)

    gram = nt(pm, pm, HIGH)
    zeros = jnp.zeros((RANK, 128 - RANK), F32)
    gl[0] = jnp.concatenate([gram[:RANK, :RANK], zeros], axis=1)
    gl[1] = jnp.concatenate([gram[RANK:, RANK:], zeros], axis=1)
    send(gl.at[1 - core], gcore, gsem_s.at[0], gsem_r.at[0], sibling)

    phl = jnp.concatenate(two_terms(pm), axis=0)
    mine = pl.ds(pl.multiple_of(core * RANK, RANK), RANK)
    theirs = pl.ds(pl.multiple_of((1 - core) * RANK, RANK), RANK)
    far_first = (2, 3, 0, 1)

    def chunk_cols(h, k):
        return pl.ds(pl.multiple_of(h * HALF + k * CHUNK, CHUNK), CHUNK)

    def swap(h, i):
        four = pl.ds(xs[i] * 4, 4)
        return remote(rloc.at[h, four, theirs], rcore.at[h, four], csem_s.at[0], csem_r.at[h * 4 + i], sibling)

    def right(h):
        for i in far_first:
            for j in (0, 2):
                k = xs[i] * 4 + j
                cols = pl.ds(pl.multiple_of(h * HALF + k * CHUNK, 2 * CHUNK), 2 * CHUNK)
                part = nn(phl, gs[:, cols]) + nn(phl, es[:, cols])
                part = part[:64] + part[64:]
                rloc[h, k] = part[:, :CHUNK]
                rloc[h, k + 1] = part[:, CHUNK:]
        for i in far_first:
            swap(h, i).start()

    right(0)

    arrived(gcore, gsem_r.at[0])
    gx[x] = gl[core] + gcore[...]
    for d in (2, 1, 3):
        send(gx.at[x], gx.at[x], gsem_s.at[1], gsem_r.at[1], dev(xs[d], y, z, core))

    right(1)

    for h in range(2):
        for i in far_first:
            swap(h, i).wait_recv()
            ks = [xs[i] * 4 + ys[j] for j in range(4)]
            for j, k in enumerate(ks):
                if i or j:
                    rs[h, k] = rloc[h, k, mine] + rcore[h, k]
                else:
                    slots[h, me] = rloc[h, k, mine] + rcore[h, k]
            for j in (2, 3, 1, 0):
                if i or j:
                    k = ks[j]
                    send(rs.at[h, k], slots.at[h, me], rsem_s.at[0], rsem_r.at[h], dev(xs[i], ys[j], z, core))

    arrived(gx.at[pl.ds(0, 3)], gsem_r.at[1])
    gz[z] = (gx[0] + gx[1]) + (gx[2] + gx[3])
    far = (4, 3, 5, 2, 6, 1, 7)
    for d in far:
        send(gz.at[z], gz.at[z], gsem_s.at[2], gsem_r.at[2], dev(x, y, zs[d], core))

    for h in range(2):
        arrived(slots.at[h, pl.ds(0, 15)], rsem_r.at[h])
        total = slots[h, 0]
        for k in range(1, 16):
            total = total + slots[h, k]
        zslots[h, z] = total
        for d in far:
            send(zslots.at[h, z], zslots.at[h, z], zsem_s.at[0], zsem_r.at[h], dev(x, y, zs[d], core))

    arrived(gz.at[pl.ds(0, 7)], gsem_r.at[2])
    gram = gz[0]
    for k in range(1, 8):
        gram = gram + gz[k]
    t = gram_schmidt(gram[:, :RANK])
    tt[core] = jnp.concatenate([t, zeros], axis=1)
    send(tt.at[core], tt.at[core], gsem_s.at[3], gsem_r.at[3], sibling)

    for h in range(2):
        arrived(zslots.at[h, pl.ds(0, 7)], zsem_r.at[h])
        total = zslots[h, 0]
        for k in range(1, 8):
            total = total + zslots[h, k]
        cols = chunk_cols(h, me)
        qn[mine, cols] = nn(t * 0.25, total, HIGH)
        for i, j in plane:
            send(qn.at[mine, cols], qn.at[mine, cols], asem_s.at[0], asem_r.at[h * 4 + x], dev(xs[i], ys[j], z, core))

    arrived(tt.at[1 - core], gsem_r.at[3])
    b = masked_pair(nn(tt[0][:, :RANK], pt, HIGH), nn(tt[1][:, :RANK], pt, HIGH)).T
    bh, bl = two_terms(b)
    bc[...] = jnp.concatenate([bh, bh, bl], axis=1)

    for h in range(2):
        for i in (0, 1, 3, 2):
            base = h * HALF + xs[i] * 4 * CHUNK
            cols = pl.ds(pl.multiple_of(base, 4 * CHUNK), 4 * CHUNK)
            fresh = pl.ds(pl.multiple_of(base, 4 * CHUNK), (4 if i else 3) * CHUNK)
            arrived(qn.at[mine, fresh], asem_r.at[h * 4 + xs[i]])
            send(qn.at[mine, cols], qn.at[mine, cols], qsem_s.at[0], qsem_r.at[0], sibling)
    arrived(qn.at[theirs], qsem_r.at[0])

    left(pslots.at[pl.ds(0, 3)], psem_s.at[0])
    left(gl.at[0], gsem_s.at[0])
    left(gx.at[pl.ds(0, 3)], gsem_s.at[1])
    left(gz.at[pl.ds(0, 7)], gsem_s.at[2])
    left(tt.at[core], gsem_s.at[3])
    left(rloc.at[:, :, theirs], csem_s.at[0])
    left(rs.at[:, pl.ds(0, 15)], rsem_s.at[0])
    left(zslots.at[:, pl.ds(0, 7)], zsem_s.at[0])
    left(qn.at[mine, pl.ds(0, 30 * CHUNK)], asem_s.at[0])
    left(qn.at[mine], qsem_s.at[0])


def output_kernel(gs, es, bc, qn, u_ref, n_ref, qo_ref, us, ns, sem):
    for l in range(2):
        pltpu.make_async_copy(qn.at[pl.ds(l * RANK, RANK), pl.ds(0, D)], qo_ref.at[l], sem.at[0]).start()
    u_rows, n_rows = u_ref.reshape(BOTH, D), n_ref.reshape(BOTH, D)
    for g, (c0, w) in enumerate(GROUPS):
        qh, ql = two_terms(qn[:, c0 : c0 + w])
        qc = jnp.concatenate([qh, ql, qh], axis=0)
        for k in range(0, w, 256):
            wide = min(256, w - k)
            cols = pl.ds(c0 + k, wide)
            prod = nn(bc[...], qc[:, k : k + wide])
            us[:, cols] = prod
            ns[:, cols] = (gs[:, cols].astype(F32) + es[:, cols].astype(F32) - prod).astype(BF)
        cols, rows = pl.ds(c0, w), pl.ds(0, BOTH)
        pltpu.make_async_copy(us.at[rows, cols], u_rows.at[:, cols], sem.at[1]).start()
        pltpu.make_async_copy(ns.at[rows, cols], n_rows.at[:, cols], sem.at[2]).start()
    rows = pl.ds(0, BOTH)
    pltpu.make_async_copy(qn.at[:, pl.ds(0, D)], qo_ref.reshape(2 * RANK, D), sem.at[0]).wait()
    pltpu.make_async_copy(us.at[rows], u_rows, sem.at[1]).wait()
    pltpu.make_async_copy(ns.at[rows], n_rows, sem.at[2]).wait()


def shards(grads, errors, q_init):
    vmem, dma = pltpu.VMEM, pltpu.SemaphoreType.DMA
    whole = (ROWS, 2, D)
    hbm = lambda a: pltpu.with_memory_space_constraint(a, pltpu.HBM)
    g = hbm(grads[0].transpose(1, 0, 2))
    e = hbm(errors[0].transpose(1, 0, 2))
    in_hbm = pl.BlockSpec(memory_space=pltpu.HBM)
    in_vmem = pl.BlockSpec(memory_space=pltpu.VMEM)
    gs, es, bc, qn = pl.pallas_call(
        reduce_kernel,
        name="reduce",
        in_specs=[in_hbm] * 3,
        out_specs=[in_vmem] * 4,
        out_shape=[
            vmem((256, PAD), BF),
            vmem((256, PAD), BF),
            vmem((256, 6 * RANK), BF),
            vmem((2 * RANK, PAD), F32),
        ],
        scratch_shapes=[
            vmem((2, RANK, D), F32),
            vmem((4, RANK, 256), F32),
            vmem((2, RANK, 128), F32),
            vmem((RANK, 128), F32),
            vmem((4, RANK, 128), F32),
            vmem((8, RANK, 128), F32),
            vmem((2, RANK, 128), F32),
            vmem((2, 16, 2 * RANK, CHUNK), F32),
            vmem((2, 16, RANK, CHUNK), F32),
            vmem((2, 16, RANK, CHUNK), F32),
            vmem((2, 16, RANK, CHUNK), F32),
            vmem((2, 8, RANK, CHUNK), F32),
            dma((9,)),
            dma((1,)), dma((1,)),
            dma((4,)), dma((4,)),
            dma((1,)), dma((8,)),
            dma((1,)), dma((2,)),
            dma((1,)), dma((2,)),
            dma((1,)), dma((8,)),
            dma((1,)), dma((1,)),
        ],
        compiler_params=pltpu.CompilerParams(
            collective_id=0, has_side_effects=True, vmem_limit_bytes=40 * 2**20
        ),
    )(g, e, hbm(q_init))
    u, n, q = pl.pallas_call(
        output_kernel,
        name="outputs",
        in_specs=[in_vmem] * 4,
        out_specs=[in_hbm] * 3,
        out_shape=[
            jax.ShapeDtypeStruct(whole, F32),
            jax.ShapeDtypeStruct(whole, BF),
            jax.ShapeDtypeStruct((2, RANK, D), F32),
        ],
        scratch_shapes=[
            vmem((256, D), F32),
            vmem((256, D), BF),
            dma((3,)),
        ],
        compiler_params=pltpu.CompilerParams(vmem_limit_bytes=40 * 2**20),
    )(gs, es, bc, qn)
    return u.transpose(1, 0, 2), n.transpose(1, 0, 2)[None], q


def solution(mesh):
    in_specs = (P("dp", None, "shard", None), P("dp", None, "shard", None), P())
    out_specs = (P(None, "shard", None), P("dp", None, "shard", None), P())
    return jax.shard_map(shards, mesh=mesh, in_specs=in_specs, out_specs=out_specs, check_vma=False)
```

profile of v0, /device:TPU:1, one launch (start us, length us, event | category | flops | bytes accessed | tf_op | source)
XLA Modules:
  0.0 42.7 jit_solution(13387687533473381338)
XLA Ops:
  0.6 39.2 %reduce.1 = (bf16[256,4096]{1,0:T(8,128)(2,1)S(1)}, bf16[256,4096]{1,0:T(8,128)(2,1)S(1)}, bf16[256,192]{1,0:T(8,128)(2,1)S(1)}, f32[64,4096]{1,0:T(8,128)S(1)}) custom-call(bf16[124,2,3968]{2,1,0:T(2,128)(2,1)} %bitcast.10, bf16[124,2,3968]{2,1,0:T(2,128)(2,1)} %bitcast.11, f32[2,32,3968]{2,1,0:T(8,128)} %q_ref.1), custom_call_target="tpu_custom_call" | custom-call | tf_op jit(solution)/shard_map/reduce/pallas_call | solution.py:294
  39.9 2.9 %outputs.1 = (f32[124,2,3968]{2,1,0:T(2,128)}, bf16[124,2,3968]{2,1,0:T(2,128)(2,1)}, f32[2,32,3968]{2,1,0:T(8,128)}) custom-call(bf16[256,4096]{1,0:T(8,128)(2,1)S(1)} %get-tuple-element.10.gs, bf16[256,4096]{1,0:T(8,128)(2,1)S(1)} %get-tuple-element.11.es, bf16[256,192]{1,0:T(8,128)(2,1)S(1)} %get-tuple-element.12.bc, f32[64,4096]{1,0:T(8,128)S(1)} %get-tuple-element.13.qn), custom_call_target="tpu_custom_call" | custom-call | tf_op jit(solution)/shard_map/outputs/pallas_call | solution.py:331
where the time goes:
time: 42.8 us; the launch traced here: 42.7 us
  Pallas kernels  42.1 us (98%)
  between operations  0.64 us (1%)
    pallas_call x1, Pallas kernels, shards(): pl.pallas_call(reduce_kernel, name='reduce', in_specs=[in_hbm] * 3, out_s...  39.2 us
    pallas_call x1, Pallas kernels, shards(): pl.pallas_call(output_kernel, name='outputs', in_specs=[in_vmem] * 4, out...  2.88 us

commit v1 on v0

--- a/solution.py
+++ b/solution.py
@@ -71,8 +71,8 @@
 
 def reduce_kernel(
     g_ref, e_ref, q_ref,
-    gs, es, bc, qn,
-    qs, pslots, gl, gcore, gx, gz, tt, rloc, rcore, rs, slots, zslots,
+    us, ns, qn,
+    gs, es, bc, qs, pslots, gl, gcore, gx, gz, tt, rloc, rcore, rs, slots, zslots,
     in_sem, psem_s, psem_r, gsem_s, gsem_r, csem_s, csem_r, rsem_s, rsem_r, zsem_s, zsem_r, asem_s, asem_r, qsem_s, qsem_r,
 ):
     shard, y = lax.axis_index("shard"), lax.axis_index("dp")
@@ -149,12 +149,6 @@
     pt = (pslots[0] + pslots[1]) + (pslots[2] + pslots[3])
     pm = masked_pair(pt, pt)
 
-    gram = nt(pm, pm, HIGH)
-    zeros = jnp.zeros((RANK, 128 - RANK), F32)
-    gl[0] = jnp.concatenate([gram[:RANK, :RANK], zeros], axis=1)
-    gl[1] = jnp.concatenate([gram[RANK:, RANK:], zeros], axis=1)
-    send(gl.at[1 - core], gcore, gsem_s.at[0], gsem_r.at[0], sibling)
-
     phl = jnp.concatenate(two_terms(pm), axis=0)
     mine = pl.ds(pl.multiple_of(core * RANK, RANK), RANK)
     theirs = pl.ds(pl.multiple_of((1 - core) * RANK, RANK), RANK)
@@ -181,12 +175,18 @@
 
     right(0)
 
+    gram = nt(pm, pm, HIGH)
+    zeros = jnp.zeros((RANK, 128 - RANK), F32)
+    gl[0] = jnp.concatenate([gram[:RANK, :RANK], zeros], axis=1)
+    gl[1] = jnp.concatenate([gram[RANK:, RANK:], zeros], axis=1)
+    send(gl.at[1 - core], gcore, gsem_s.at[0], gsem_r.at[0], sibling)
+
+    right(1)
+
     arrived(gcore, gsem_r.at[0])
     gx[x] = gl[core] + gcore[...]
     for d in (2, 1, 3):
         send(gx.at[x], gx.at[x], gsem_s.at[1], gsem_r.at[1], dev(xs[d], y, z, core))
-
-    right(1)
 
     for h in range(2):
         for i in far_first:
@@ -225,13 +225,17 @@
     tt[core] = jnp.concatenate([t, zeros], axis=1)
     send(tt.at[core], tt.at[core], gsem_s.at[3], gsem_r.at[3], sibling)
 
+    th, tl = two_terms(t * 0.25)
+    t_terms = jnp.concatenate([th, th, tl], axis=1)
+
     for h in range(2):
         arrived(zslots.at[h, pl.ds(0, 7)], zsem_r.at[h])
         total = zslots[h, 0]
         for k in range(1, 8):
             total = total + zslots[h, k]
         cols = chunk_cols(h, me)
-        qn[mine, cols] = nn(t * 0.25, total, HIGH)
+        rh, rl = two_terms(total)
+        qn[mine, cols] = nn(t_terms, jnp.concatenate([rh, rl, rh], axis=0))
         for i, j in plane:
             send(qn.at[mine, cols], qn.at[mine, cols], asem_s.at[0], asem_r.at[h * 4 + x], dev(xs[i], ys[j], z, core))
 
@@ -240,14 +244,31 @@
     bh, bl = two_terms(b)
     bc[...] = jnp.concatenate([bh, bh, bl], axis=1)
 
-    for h in range(2):
-        for i in (0, 1, 3, 2):
-            base = h * HALF + xs[i] * 4 * CHUNK
-            cols = pl.ds(pl.multiple_of(base, 4 * CHUNK), 4 * CHUNK)
-            fresh = pl.ds(pl.multiple_of(base, 4 * CHUNK), (4 if i else 3) * CHUNK)
-            arrived(qn.at[mine, fresh], asem_r.at[h * 4 + xs[i]])
-            send(qn.at[mine, cols], qn.at[mine, cols], qsem_s.at[0], qsem_r.at[0], sibling)
-    arrived(qn.at[theirs], qsem_r.at[0])
+    def group(h, i, chunks=4):
+        return pl.ds(pl.multiple_of(h * HALF + xs[i] * 4 * CHUNK, 4 * CHUNK), chunks * CHUNK)
+
+    def pass_on(h, i):
+        arrived(qn.at[mine, group(h, i, 4 if i else 3)], asem_r.at[h * 4 + xs[i]])
+        cols = group(h, i)
+        send(qn.at[mine, cols], qn.at[mine, cols], qsem_s.at[0], qsem_r.at[h * 4 + i], sibling)
+
+    def update(h, i):
+        arrived(qn.at[theirs, group(h, i)], qsem_r.at[h * 4 + i])
+        for part in range(2):
+            cols = pl.ds(pl.multiple_of(h * HALF + xs[i] * 4 * CHUNK + part * 256, 256), 256)
+            qh, ql = two_terms(qn[:, cols])
+            prod = nn(bc[...], jnp.concatenate([qh, ql, qh], axis=0))
+            us[:, cols] = prod
+            ns[:, cols] = (gs[:, cols].astype(F32) + es[:, cols].astype(F32) - prod).astype(BF)
+
+    near_first = (0, 1, 3, 2)
+    for i in near_first:
+        pass_on(0, i)
+    for i in near_first:
+        update(0, i)
+        pass_on(1, i)
+    for i in near_first:
+        update(1, i)
 
     left(pslots.at[pl.ds(0, 3)], psem_s.at[0])
     left(gl.at[0], gsem_s.at[0])
@@ -261,26 +282,18 @@
     left(qn.at[mine], qsem_s.at[0])
 
 
-def output_kernel(gs, es, bc, qn, u_ref, n_ref, qo_ref, us, ns, sem):
-    for l in range(2):
-        pltpu.make_async_copy(qn.at[pl.ds(l * RANK, RANK), pl.ds(0, D)], qo_ref.at[l], sem.at[0]).start()
-    u_rows, n_rows = u_ref.reshape(BOTH, D), n_ref.reshape(BOTH, D)
-    for g, (c0, w) in enumerate(GROUPS):
-        qh, ql = two_terms(qn[:, c0 : c0 + w])
-        qc = jnp.concatenate([qh, ql, qh], axis=0)
-        for k in range(0, w, 256):
-            wide = min(256, w - k)
-            cols = pl.ds(c0 + k, wide)
-            prod = nn(bc[...], qc[:, k : k + wide])
-            us[:, cols] = prod
-            ns[:, cols] = (gs[:, cols].astype(F32) + es[:, cols].astype(F32) - prod).astype(BF)
-        cols, rows = pl.ds(c0, w), pl.ds(0, BOTH)
-        pltpu.make_async_copy(us.at[rows, cols], u_rows.at[:, cols], sem.at[1]).start()
-        pltpu.make_async_copy(ns.at[rows, cols], n_rows.at[:, cols], sem.at[2]).start()
+def output_kernel(us, ns, qn, u_ref, n_ref, qo_ref, sem):
+    u_rows, n_rows, q_rows = u_ref.reshape(BOTH, D), n_ref.reshape(BOTH, D), qo_ref.reshape(2 * RANK, D)
     rows = pl.ds(0, BOTH)
-    pltpu.make_async_copy(qn.at[:, pl.ds(0, D)], qo_ref.reshape(2 * RANK, D), sem.at[0]).wait()
-    pltpu.make_async_copy(us.at[rows], u_rows, sem.at[1]).wait()
-    pltpu.make_async_copy(ns.at[rows], n_rows, sem.at[2]).wait()
+    for c0, w in GROUPS:
+        cols = pl.ds(c0, w)
+        pltpu.make_async_copy(us.at[rows, cols], u_rows.at[:, cols], sem.at[0]).start()
+        pltpu.make_async_copy(ns.at[rows, cols], n_rows.at[:, cols], sem.at[1]).start()
+        pltpu.make_async_copy(qn.at[:, cols], q_rows.at[:, cols], sem.at[2]).start()
+    cols = pl.ds(0, D)
+    pltpu.make_async_copy(us.at[rows, cols], u_rows, sem.at[0]).wait()
+    pltpu.make_async_copy(ns.at[rows, cols], n_rows, sem.at[1]).wait()
+    pltpu.make_async_copy(qn.at[:, cols], q_rows, sem.at[2]).wait()
 
 
 def shards(grads, errors, q_init):
@@ -291,18 +304,20 @@
     e = hbm(errors[0].transpose(1, 0, 2))
     in_hbm = pl.BlockSpec(memory_space=pltpu.HBM)
     in_vmem = pl.BlockSpec(memory_space=pltpu.VMEM)
-    gs, es, bc, qn = pl.pallas_call(
+    us, ns, qn = pl.pallas_call(
         reduce_kernel,
         name="reduce",
         in_specs=[in_hbm] * 3,
-        out_specs=[in_vmem] * 4,
+        out_specs=[in_vmem] * 3,
         out_shape=[
+            vmem((256, PAD), F32),
+            vmem((256, PAD), BF),
+            vmem((2 * RANK, PAD), F32),
+        ],
+        scratch_shapes=[
             vmem((256, PAD), BF),
             vmem((256, PAD), BF),
             vmem((256, 6 * RANK), BF),
-            vmem((2 * RANK, PAD), F32),
-        ],
-        scratch_shapes=[
             vmem((2, RANK, D), F32),
             vmem((4, RANK, 256), F32),
             vmem((2, RANK, 128), F32),
@@ -322,7 +337,7 @@
             dma((1,)), dma((2,)),
             dma((1,)), dma((2,)),
             dma((1,)), dma((8,)),
-            dma((1,)), dma((1,)),
+            dma((1,)), dma((8,)),
         ],
         compiler_params=pltpu.CompilerParams(
             collective_id=0, has_side_effects=True, vmem_limit_bytes=40 * 2**20
@@ -331,7 +346,7 @@
     u, n, q = pl.pallas_call(
         output_kernel,
         name="outputs",
-        in_specs=[in_vmem] * 4,
+        in_specs=[in_vmem] * 3,
         out_specs=[in_hbm] * 3,
         out_shape=[
             jax.ShapeDtypeStruct(whole, F32),
@@ -339,12 +354,10 @@
             jax.ShapeDtypeStruct((2, RANK, D), F32),
         ],
         scratch_shapes=[
-            vmem((256, D), F32),
-            vmem((256, D), BF),
             dma((3,)),
         ],
         compiler_params=pltpu.CompilerParams(vmem_limit_bytes=40 * 2**20),
-    )(gs, es, bc, qn)
+    )(us, ns, qn)
     return u.transpose(1, 0, 2), n.transpose(1, 0, 2)[None], q
 
 

time: 42.8 us -> 43.9 us (1.026)
  Pallas kernels: 42.1 us -> 43.2 us
    pallas_call x1, Pallas kernels: 39.2 us -> 40.3 us  [shards(): pl.pallas_call(reduce_kernel, name='reduce', in_specs=[in_hbm] * 3, out_s...]
where the time goes in v1:
time: 43.9 us; the launch traced here: 43.8 us
  Pallas kernels  43.2 us (98%)
  between operations  0.64 us (1%)
    pallas_call x1, Pallas kernels, shards(): pl.pallas_call(reduce_kernel, name='reduce', in_specs=[in_hbm] * 3, out_s...  40.3 us
    pallas_call x1, Pallas kernels, shards(): pl.pallas_call(output_kernel, name='outputs', in_specs=[in_vmem] * 3, out...  2.86 us

profile of v1, /device:TPU:1, one launch (start us, length us, event | category | flops | bytes accessed | tf_op | source)
XLA Modules:
  0.0 43.8 jit_solution(18174219570186151333)
XLA Ops:
  0.6 40.3 %reduce.1 = (f32[256,4096]{1,0:T(8,128)S(1)}, bf16[256,4096]{1,0:T(8,128)(2,1)S(1)}, f32[64,4096]{1,0:T(8,128)S(1)}) custom-call(bf16[124,2,3968]{2,1,0:T(2,128)(2,1)} %bitcast.10, bf16[124,2,3968]{2,1,0:T(2,128)(2,1)} %bitcast.11, f32[2,32,3968]{2,1,0:T(8,128)} %q_ref.1), custom_call_target="tpu_custom_call" | custom-call | tf_op jit(solution)/shard_map/reduce/pallas_call | solution.py:307
  41.0 2.9 %outputs.1 = (f32[124,2,3968]{2,1,0:T(2,128)}, bf16[124,2,3968]{2,1,0:T(2,128)(2,1)}, f32[2,32,3968]{2,1,0:T(8,128)}) custom-call(f32[256,4096]{1,0:T(8,128)S(1)} %get-tuple-element.9.us, bf16[256,4096]{1,0:T(8,128)(2,1)S(1)} %get-tuple-element.10.ns, f32[64,4096]{1,0:T(8,128)S(1)} %get-tuple-element.11.qn), custom_call_target="tpu_custom_call" | custom-call | tf_op jit(solution)/shard_map/outputs/pallas_call | solution.py:346

commit v2 on v0

--- a/solution.py
+++ b/solution.py
@@ -17,6 +17,7 @@
 PAD = 4096
 HALF, CHUNK = PAD // 2, 128
 GROUPS = ((0, 1024), (1024, 1024), (2048, 1024), (3072, 896))
+OUT_GROUPS = ((0, 256), (256, 768), (1024, 1024), (2048, 1024), (3072, 896))
 EPS = 1e-06
 
 
@@ -158,7 +159,7 @@
     phl = jnp.concatenate(two_terms(pm), axis=0)
     mine = pl.ds(pl.multiple_of(core * RANK, RANK), RANK)
     theirs = pl.ds(pl.multiple_of((1 - core) * RANK, RANK), RANK)
-    far_first = (2, 3, 0, 1)
+    far, close = (2, 3), (0, 1)
 
     def chunk_cols(h, k):
         return pl.ds(pl.multiple_of(h * HALF + k * CHUNK, CHUNK), CHUNK)
@@ -167,8 +168,8 @@
         four = pl.ds(xs[i] * 4, 4)
         return remote(rloc.at[h, four, theirs], rcore.at[h, four], csem_s.at[0], csem_r.at[h * 4 + i], sibling)
 
-    def right(h):
-        for i in far_first:
+    def right(h, group):
+        for i in group:
             for j in (0, 2):
                 k = xs[i] * 4 + j
                 cols = pl.ds(pl.multiple_of(h * HALF + k * CHUNK, 2 * CHUNK), 2 * CHUNK)
@@ -176,20 +177,11 @@
                 part = part[:64] + part[64:]
                 rloc[h, k] = part[:, :CHUNK]
                 rloc[h, k + 1] = part[:, CHUNK:]
-        for i in far_first:
+        for i in group:
             swap(h, i).start()
 
-    right(0)
-
-    arrived(gcore, gsem_r.at[0])
-    gx[x] = gl[core] + gcore[...]
-    for d in (2, 1, 3):
-        send(gx.at[x], gx.at[x], gsem_s.at[1], gsem_r.at[1], dev(xs[d], y, z, core))
-
-    right(1)
-
-    for h in range(2):
-        for i in far_first:
+    def scatter(h, group):
+        for i in group:
             swap(h, i).wait_recv()
             ks = [xs[i] * 4 + ys[j] for j in range(4)]
             for j, k in enumerate(ks):
@@ -202,10 +194,25 @@
                     k = ks[j]
                     send(rs.at[h, k], slots.at[h, me], rsem_s.at[0], rsem_r.at[h], dev(xs[i], ys[j], z, core))
 
+    right(0, far)
+    right(0, close)
+
+    arrived(gcore, gsem_r.at[0])
+    gx[x] = gl[core] + gcore[...]
+    for d in (2, 1, 3):
+        send(gx.at[x], gx.at[x], gsem_s.at[1], gsem_r.at[1], dev(xs[d], y, z, core))
+
+    right(1, far)
+    scatter(0, far)
+    right(1, close)
+    scatter(0, close)
+    scatter(1, far)
+    scatter(1, close)
+
     arrived(gx.at[pl.ds(0, 3)], gsem_r.at[1])
     gz[z] = (gx[0] + gx[1]) + (gx[2] + gx[3])
-    far = (4, 3, 5, 2, 6, 1, 7)
-    for d in far:
+    around = (4, 3, 5, 2, 6, 1, 7)
+    for d in around:
         send(gz.at[z], gz.at[z], gsem_s.at[2], gsem_r.at[2], dev(x, y, zs[d], core))
 
     for h in range(2):
@@ -214,7 +221,7 @@
         for k in range(1, 16):
             total = total + slots[h, k]
         zslots[h, z] = total
-        for d in far:
+        for d in around:
             send(zslots.at[h, z], zslots.at[h, z], zsem_s.at[0], zsem_r.at[h], dev(x, y, zs[d], core))
 
     arrived(gz.at[pl.ds(0, 7)], gsem_r.at[2])
@@ -225,13 +232,17 @@
     tt[core] = jnp.concatenate([t, zeros], axis=1)
     send(tt.at[core], tt.at[core], gsem_s.at[3], gsem_r.at[3], sibling)
 
+    th, tl = two_terms(t * 0.25)
+    t_terms = jnp.concatenate([th, th, tl], axis=1)
+
     for h in range(2):
         arrived(zslots.at[h, pl.ds(0, 7)], zsem_r.at[h])
         total = zslots[h, 0]
         for k in range(1, 8):
             total = total + zslots[h, k]
         cols = chunk_cols(h, me)
-        qn[mine, cols] = nn(t * 0.25, total, HIGH)
+        rh, rl = two_terms(total)
+        qn[mine, cols] = nn(t_terms, jnp.concatenate([rh, rl, rh], axis=0))
         for i, j in plane:
             send(qn.at[mine, cols], qn.at[mine, cols], asem_s.at[0], asem_r.at[h * 4 + x], dev(xs[i], ys[j], z, core))
 
@@ -265,7 +276,7 @@
     for l in range(2):
         pltpu.make_async_copy(qn.at[pl.ds(l * RANK, RANK), pl.ds(0, D)], qo_ref.at[l], sem.at[0]).start()
     u_rows, n_rows = u_ref.reshape(BOTH, D), n_ref.reshape(BOTH, D)
-    for g, (c0, w) in enumerate(GROUPS):
+    for c0, w in OUT_GROUPS:
         qh, ql = two_terms(qn[:, c0 : c0 + w])
         qc = jnp.concatenate([qh, ql, qh], axis=0)
         for k in range(0, w, 256):

time: 42.8 us -> 42.7 us (level)
  no operation moved by 1% of the time
where the time goes in v2:
time: 42.7 us; the launch traced here: 42.6 us
  Pallas kernels  42 us (98%)
  between operations  0.64 us (1%)
    pallas_call x1, Pallas kernels, shards(): pl.pallas_call(reduce_kernel, name='reduce', in_specs=[in_hbm] * 3, out_s...  39 us
    pallas_call x1, Pallas kernels, shards(): pl.pallas_call(output_kernel, name='outputs', in_specs=[in_vmem] * 4, out...  2.93 us

profile of v2, /device:TPU:1, one launch (start us, length us, event | category | flops | bytes accessed | tf_op | source)
XLA Modules:
  0.0 42.6 jit_solution(5158208827159262936)
XLA Ops:
  0.6 39.0 %reduce.1 = (bf16[256,4096]{1,0:T(8,128)(2,1)S(1)}, bf16[256,4096]{1,0:T(8,128)(2,1)S(1)}, bf16[256,192]{1,0:T(8,128)(2,1)S(1)}, f32[64,4096]{1,0:T(8,128)S(1)}) custom-call(bf16[124,2,3968]{2,1,0:T(2,128)(2,1)} %bitcast.10, bf16[124,2,3968]{2,1,0:T(2,128)(2,1)} %bitcast.11, f32[2,32,3968]{2,1,0:T(8,128)} %q_ref.1), custom_call_target="tpu_custom_call" | custom-call | tf_op jit(solution)/shard_map/reduce/pallas_call | solution.py:305
  39.7 2.9 %outputs.1 = (f32[124,2,3968]{2,1,0:T(2,128)}, bf16[124,2,3968]{2,1,0:T(2,128)(2,1)}, f32[2,32,3968]{2,1,0:T(8,128)}) custom-call(bf16[256,4096]{1,0:T(8,128)(2,1)S(1)} %get-tuple-element.10.gs, bf16[256,4096]{1,0:T(8,128)(2,1)S(1)} %get-tuple-element.11.es, bf16[256,192]{1,0:T(8,128)(2,1)S(1)} %get-tuple-element.12.bc, f32[64,4096]{1,0:T(8,128)S(1)} %get-tuple-element.13.qn), custom_call_target="tpu_custom_call" | custom-call | tf_op jit(solution)/shard_map/outputs/pallas_call | solution.py:342
